TPU v7x, 32 devices: a whole 2x2x4 slice. The times are simulated.
32 devices in a mesh: groups: 2 (over x), rows: 8 (over z, y), cols: 2 (over core).
Axes of the slice: x: 2, y: 2, z: 4, core: 2. Of those that a mesh axis runs over, the one named last changes fastest.
Arguments:
- rhs_field: bfloat16 [64, 8192], P(None, ('groups', 'rows', 'cols')), parts along dimension 1, may hold values from -6 to 6
- far_left: bfloat16 [32, 64, 64, 256], P(('groups', 'rows', 'cols')), parts along dimension 0, may hold values from -0.09375 to 0.09375
- far_right: bfloat16 [32, 64, 64, 256], P(('groups', 'rows', 'cols')), parts along dimension 0, may hold values from -0.375 to 0.375
- far_rows: int32 [32, 64], P(('groups', 'rows', 'cols')), parts along dimension 0, may hold values from 0 to 15, as said below
- far_cols: int32 [32, 64], P(('groups', 'rows', 'cols')), parts along dimension 0, may hold values from 0 to 15, as said below
- far_ranks: int32 [32, 64], P(('groups', 'rows', 'cols')), parts along dimension 0, may hold values from 8 to 64
- far_counts: int32 [32], P(('groups', 'rows', 'cols')), parts along dimension 0, may hold values from 0 to 64, as said below
- near_blocks: bfloat16 [32, 8, 256, 256], P(('groups', 'rows', 'cols')), parts along dimension 0, may hold values from -0.125 to 0.125
- near_rows: int32 [32, 8], P(('groups', 'rows', 'cols')), parts along dimension 0, may hold values from 0 to 15, as said below
- near_cols: int32 [32, 8], P(('groups', 'rows', 'cols')), parts along dimension 0, may hold values from 0 to 15, as said below
Outputs:
- product: float32 [64, 8192], P(None, ('groups', 'rows', 'cols')), parts along dimension 1
There are 2 independent parts, one for each index of `groups`. A program takes and returns all parts, laid end to end along the dimension named above; each array names one. Nothing has to cross between parts.
Inputs may be any that keep to these rules, and one draw needn't show every extreme that they name: `far_rows`: entry [d, s] divided by 2, rounded down, equals d divided by 2, rounded down. `far_cols`: entry [d, s] modulo 2 equals d modulo 2. `far_counts`: entries d and (d + 8) modulo 16 sum to 64. `near_rows`: entry [d, s] divided by 2, rounded down, equals d divided by 2, rounded down. `near_cols`: entry [d, s] modulo 2 equals d modulo 2, and entry [d, s] divided by 2, rounded down, differs by at most one from d divided by 2, rounded down.
All inputs are finite; a program needn't handle non-finite values.
Results may differ from a plain program's by a relative error of at most 0.0014.
Values may be sent and summed in bfloat16 or wider, within the bound.
A program may use at most 64 MiB of HBM per device.

v0:
```python
import jax
import jax.numpy as jnp
from jax import lax
from jax.sharding import PartitionSpec as P


def row_fold(contribution, row_ids, col_count):
    targets = jnp.arange(col_count, dtype=jnp.int32)
    chosen = (row_ids[:, None] % col_count == targets[None, :]).astype(jnp.float32)
    return jnp.sum(contribution[:, :, None, :] * chosen[None, :, :, None], axis=1)


def far_terms(column_blocks, left, right, row_ids, col_ids, rank_ids, live_count, col_count):
    group_width = 8
    rhs_count = column_blocks.shape[0]
    leaf_width = column_blocks.shape[2]
    rank_width = left.shape[1]
    turns = (live_count + group_width - 1) // group_width
    rank_range = jnp.arange(rank_width, dtype=jnp.int32)
    slot_range = jnp.arange(group_width, dtype=jnp.int32)

    def accumulate(turn_index, running):
        first_slot = turn_index * group_width
        left_group = lax.dynamic_slice_in_dim(left, first_slot, group_width, 0)
        right_group = lax.dynamic_slice_in_dim(right, first_slot, group_width, 0)
        row_group = lax.dynamic_slice_in_dim(row_ids, first_slot, group_width, 0)
        col_group = lax.dynamic_slice_in_dim(col_ids, first_slot, group_width, 0)
        rank_group = lax.dynamic_slice_in_dim(rank_ids, first_slot, group_width, 0)
        x_pieces = jnp.take(column_blocks, col_group // col_count, axis=1)
        scores = jnp.einsum(
            "hsn,skn->hsk", x_pieces, right_group, preferred_element_type=jnp.float32
        )
        slot_live = first_slot + slot_range < live_count
        kept_mask = slot_live[:, None] & (rank_range[None, :] < rank_group[:, None])
        coefficients = jnp.where(kept_mask[None], scores, 0.0).astype(jnp.bfloat16)
        contribution = jnp.einsum(
            "hsk,skn->hsn", coefficients, left_group, preferred_element_type=jnp.float32
        )
        return running + row_fold(contribution, row_group, col_count)

    initial = jnp.zeros((rhs_count, col_count, leaf_width), jnp.float32)
    return lax.fori_loop(0, turns, accumulate, initial)


def on_device(
    rhs_field,
    far_left,
    far_right,
    far_rows,
    far_cols,
    far_ranks,
    far_counts,
    near_blocks,
    near_rows,
    near_cols,
):
    col_count = lax.axis_size("cols")
    row_count = lax.axis_size("rows")
    rhs_count = rhs_field.shape[0]
    leaf_width = rhs_field.shape[1]
    left_store = far_left[0]
    right_store = far_right[0]
    row_store = far_rows[0]
    col_store = far_cols[0]
    rank_store = far_ranks[0]
    count_here = far_counts[0]
    near_store = near_blocks[0]
    near_row_ids = near_rows[0]
    near_keys = near_cols[0] // col_count
    gathered = lax.all_gather(rhs_field, "rows", axis=1, tiled=True)
    column_blocks = gathered.reshape(rhs_count, row_count, leaf_width)
    near_pieces = jnp.take(column_blocks, near_keys, axis=1)
    near_products = jnp.einsum(
        "hsn,snm->hsm", near_pieces, near_store, preferred_element_type=jnp.float32
    )
    near_partial = row_fold(near_products, near_row_ids, col_count)
    far_partial = far_terms(
        column_blocks,
        left_store,
        right_store,
        row_store,
        col_store,
        rank_store,
        count_here,
        col_count,
    )
    partial_value = near_partial + far_partial
    owned = lax.psum_scatter(partial_value, "cols", scatter_dimension=1, tiled=True)
    return owned.reshape(rhs_count, leaf_width)


def solution(mesh):
    placed = (
        P(None, ("groups", "rows", "cols")),
        P(("groups", "rows", "cols"), None, None, None),
        P(("groups", "rows", "cols"), None, None, None),
        P(("groups", "rows", "cols"), None),
        P(("groups", "rows", "cols"), None),
        P(("groups", "rows", "cols"), None),
        P(("groups", "rows", "cols")),
        P(("groups", "rows", "cols"), None, None, None),
        P(("groups", "rows", "cols"), None),
        P(("groups", "rows", "cols"), None),
    )
    return jax.shard_map(
        on_device,
        mesh=mesh,
        in_specs=placed,
        out_specs=P(None, ("groups", "rows", "cols")),
        check_vma=False,
    )
```

profile of v0, /device:TPU:0, one launch (start us, length us, event | category | flops | bytes accessed | tf_op | source)
XLA Modules:
  0.0 98.3 jit_solution(18263187788749936077)
XLA Ops:
  6.5 0.0 copy-start
  6.5 0.0 reduce-scatter.2.cloned.1.call-start
  7.3 0.7 fusion.33
  8.0 0.7 compare_and_fusion.1
  8.6 32.7 %all_gather.3 = bf16[64,2048]{1,0:T(8,128)(2,1)S(1)} all-gather(bf16[64,256]{1,0:T(8,128)(2,1)} %param.12), channel_id=1, replica_groups=mesh['groups'=2,'rows'=8,'cols'=2] {'rows'}, dimensions={1}, use_global_device_ids=true | all-gather | bytes 294912 | tf_op jit(solution)/shard_map/all_gather | solution.py:70
  41.5 0.0 copy-start.2
  41.5 0.6 gather_fusion.1
  42.1 0.0 copy-done
  42.1 0.3 convolution_bitcast_fusion.1
  42.4 0.3 copy.32
  42.7 0.0 copy-done.2
  42.8 0.4 multiply_reduce_fusion.1
  43.2 0.1 add.105
  43.3 0.6 copy.34
  43.9 0.0 reduce-scatter.2.cloned.1.call-update
  44.0 47.5 %reduce-scatter.2.cloned.1.call-done = f32[64,1,256]{2,0,1:T(8,128)} async-done(((f32[64,2,256]{2,0,1:T(8,128)}), f32[64,1,256]{2,0,1:T(8,128)}) %reduce-scatter.2.cloned.1.call-update) | async-done | bytes 65552 | tf_op jit(solution)/shard_map/reduce_scatter | solution.py:88
  (6 shorter events, 0.1 us)
Async XLA Ops:
  6.5 35.5 %copy-start = (bf16[1,8,256,256]{3,2,1,0:T(8,128)(2,1)S(1)}, bf16[1,8,256,256]{3,2,1,0:T(8,128)(2,1)}, u32[]{:S(2)}) copy-start(bf16[1,8,256,256]{3,2,1,0:T(8,128)(2,1)} %param.19) | copy-start | bytes 3145732
  6.5 84.9 %reduce-scatter.2.cloned.1.call-start = ((), (), s32[]{:S(2)}) async-start(), calls=%async_computation.1 | async-start | bytes 196608 | tf_op jit(solution)/shard_map/reduce_scatter | solution.py:88
  41.5 1.3 %copy-start.2 = (s32[1,8]{1,0:T(1,128)S(1)}, s32[1,8]{1,0:T(1,128)}, u32[]{:S(2)}) copy-start(s32[1,8]{1,0:T(1,128)} %param.20) | copy-start | bytes 100
Sparse Core Ops, SparseCore 0:
  44.1 47.3 reduce-scatter.1
where the time goes:
time: 100 us; the launch traced here: 98.3 us
  waiting for transfers between devices  47.5 us (48%)
  blocking collectives  32.7 us (33%)
  between operations  14.3 us (14%)
  other arithmetic  1.85 us (2%)
  local copies, waits for them, and re-layouts  1.58 us (2%)
    reduce_scatter x1, waiting for transfers between devices, on_device(): lax.psum_scatter(partial_value, 'cols', scatter_dimension=1, tiled=True)  47.5 us
    all_gather x1, blocking collectives, on_device(): gathered = lax.all_gather(rhs_field, 'rows', axis=1, tiled=True)  32.7 us
  transfers between devices with their start and end apart: 1, of which 1 were waited for; matrix products, arithmetic and copies ran while one was open for 0% of the time, Pallas kernels for 0%

commit v1 on v0

v1 whole, which is shorter than its diff:
```python
import functools

import jax
import jax.numpy as jnp
from jax import lax
from jax.experimental import pallas as pl
from jax.experimental.pallas import tpu as pltpu
from jax.sharding import PartitionSpec as P

MESH = pl.DeviceIdType.MESH


def kernel(
    n_rows,
    n_cols,
    x_ref,
    left_ref,
    right_ref,
    far_rows_ref,
    far_cols_ref,
    far_ranks_ref,
    far_counts_ref,
    near_ref,
    near_rows_ref,
    near_cols_ref,
    out_ref,
    x_all,
    left,
    right,
    near,
    outgoing,
    incoming,
    local_sem,
    send_sem,
    recv_sem,
    pair_sem,
):
    row = lax.axis_index("rows")
    col = lax.axis_index("cols")
    far_slots, rank, leaf = right.shape
    near_slots = near.shape[0]
    rhs = x_ref.shape[0]

    loads = [
        pltpu.make_async_copy(x_ref, x_all.at[row], local_sem.at[0]),
        pltpu.make_async_copy(right_ref.at[0], right, local_sem.at[1]),
        pltpu.make_async_copy(near_ref.at[0], near, local_sem.at[2]),
        pltpu.make_async_copy(left_ref.at[0], left, local_sem.at[3]),
    ]
    for load in loads:
        load.start()

    barrier = pltpu.get_barrier_semaphore()
    for offset in range(1, n_rows):
        peer = lax.rem(row + offset, n_rows)
        pl.semaphore_signal(barrier, inc=1, device_id={"rows": peer}, device_id_type=MESH)
    pl.semaphore_signal(barrier, inc=1, device_id={"cols": 1 - col}, device_id_type=MESH)
    pl.semaphore_wait(barrier, n_rows)

    sends = []
    for offset in range(1, n_rows):
        peer = lax.rem(row + offset, n_rows)
        copy = pltpu.make_async_remote_copy(
            src_ref=x_ref,
            dst_ref=x_all.at[row],
            send_sem=send_sem.at[offset],
            recv_sem=recv_sem.at[offset],
            device_id={"rows": peer},
            device_id_type=MESH,
        )
        copy.start()
        sends.append(copy)
    for offset in range(1, n_rows):
        source = lax.rem(row + n_rows - offset, n_rows)
        pltpu.make_async_remote_copy(
            src_ref=x_ref,
            dst_ref=x_all.at[source],
            send_sem=send_sem.at[offset],
            recv_sem=recv_sem.at[offset],
            device_id={"rows": source},
            device_id_type=MESH,
        ).wait_recv()
    for load in loads:
        load.wait()

    live = far_counts_ref[0]
    acc = jnp.zeros((2 * rhs, leaf), jnp.float32)
    for slot in range(near_slots):
        piece = x_all[near_cols_ref[0, slot] // n_cols]
        mine = near_rows_ref[0, slot] % n_cols == col
        empty = jnp.zeros_like(piece)
        both = jnp.concatenate([jnp.where(mine, piece, empty), jnp.where(mine, empty, piece)], axis=0)
        acc += jnp.dot(both, near[slot], preferred_element_type=jnp.float32)

    width = 2 * rank
    lane = lax.broadcasted_iota(jnp.int32, (rhs, width), 1)
    first = lane < rank
    group = 4
    for start in range(0, far_slots, group):
        halves = []
        for a in range(start, start + group, 2):
            b = a + 1
            pieces = jnp.concatenate(
                [x_all[far_cols_ref[0, a] // n_cols], x_all[far_cols_ref[0, b] // n_cols]], axis=0
            )
            weights = right[a : a + 2].reshape(width, leaf)
            scores = lax.dot_general(
                pieces, weights, (((1,), (1,)), ((), ())), preferred_element_type=jnp.float32
            )
            scores = jnp.where(first, scores[:rhs], scores[rhs:])
            end_a = jnp.where(a < live, far_ranks_ref[0, a], 0)
            end_b = jnp.where(b < live, far_ranks_ref[0, b], 0) + rank
            mine_a = far_rows_ref[0, a] % n_cols == col
            mine_b = far_rows_ref[0, b] % n_cols == col
            own = lane < jnp.where(first, jnp.where(mine_a, end_a, 0), jnp.where(mine_b, end_b, 0))
            other = lane < jnp.where(first, jnp.where(mine_a, 0, end_a), jnp.where(mine_b, 0, end_b))
            halves.append(
                jnp.concatenate(
                    [jnp.where(own, scores, 0.0), jnp.where(other, scores, 0.0)], axis=0
                ).astype(jnp.bfloat16)
            )
        coefficients = jnp.concatenate(halves, axis=1)
        acc += jnp.dot(
            coefficients,
            left[start : start + group].reshape(group * rank, leaf),
            preferred_element_type=jnp.float32,
        )

    outgoing[...] = acc[rhs:]
    exchange = pltpu.make_async_remote_copy(
        src_ref=outgoing,
        dst_ref=incoming,
        send_sem=pair_sem.at[0],
        recv_sem=pair_sem.at[1],
        device_id={"cols": 1 - col},
        device_id_type=MESH,
    )
    exchange.start()
    for copy in sends:
        copy.wait_send()
    exchange.wait()
    out_ref[...] = acc[:rhs] + incoming[...]


def on_device(
    n_rows,
    n_cols,
    rhs_field,
    far_left,
    far_right,
    far_rows,
    far_cols,
    far_ranks,
    far_counts,
    near_blocks,
    near_rows,
    near_cols,
):
    rhs, leaf = rhs_field.shape
    anywhere = pl.BlockSpec(memory_space=pl.ANY)
    scalars = pl.BlockSpec(memory_space=pltpu.SMEM)
    return pl.pallas_call(
        functools.partial(kernel, n_rows, n_cols),
        out_shape=jax.ShapeDtypeStruct((rhs, leaf), jnp.float32),
        in_specs=[
            anywhere,
            anywhere,
            anywhere,
            scalars,
            scalars,
            scalars,
            scalars,
            anywhere,
            scalars,
            scalars,
        ],
        out_specs=pl.BlockSpec(memory_space=pltpu.VMEM),
        scratch_shapes=[
            pltpu.VMEM((n_rows, rhs, leaf), jnp.bfloat16),
            pltpu.VMEM(far_left.shape[1:], jnp.bfloat16),
            pltpu.VMEM(far_right.shape[1:], jnp.bfloat16),
            pltpu.VMEM(near_blocks.shape[1:], jnp.bfloat16),
            pltpu.VMEM((rhs, leaf), jnp.float32),
            pltpu.VMEM((rhs, leaf), jnp.float32),
            pltpu.SemaphoreType.DMA((4,)),
            pltpu.SemaphoreType.DMA((n_rows,)),
            pltpu.SemaphoreType.DMA((n_rows,)),
            pltpu.SemaphoreType.DMA((2,)),
        ],
        compiler_params=pltpu.CompilerParams(
            collective_id=0, has_side_effects=True, vmem_limit_bytes=32 * 1024 * 1024
        ),
    )(
        rhs_field,
        far_left,
        far_right,
        far_rows,
        far_cols,
        far_ranks,
        far_counts,
        near_blocks,
        near_rows,
        near_cols,
    )


def solution(mesh):
    split = ("groups", "rows", "cols")
    placed = (
        P(None, split),
        P(split, None, None, None),
        P(split, None, None, None),
        P(split, None),
        P(split, None),
        P(split, None),
        P(split),
        P(split, None, None, None),
        P(split, None),
        P(split, None),
    )
    return jax.shard_map(
        functools.partial(on_device, mesh.shape["rows"], mesh.shape["cols"]),
        mesh=mesh,
        in_specs=placed,
        out_specs=P(None, split),
        check_vma=False,
    )
```

time: 100 us -> 25.1 us (0.25); the launches traced: 98.3 us -> 24.8 us
  waiting for transfers between devices: 47.5 us -> 0 us
  blocking collectives: 32.7 us -> 0 us
  Pallas kernels: 0 us -> 15.1 us
  between operations: 14.3 us -> 0.68 us
  local copies, waits for them, and re-layouts: 1.58 us -> 9.06 us
  other arithmetic: 1.85 us -> 0 us
    reduce_scatter x1 -> x0, waiting for transfers between devices: 47.5 us -> none  [on_device(): lax.psum_scatter(partial_value, 'cols', scatter_dimension=1, tiled=True)]
    all_gather x1 -> x0, blocking collectives: 32.7 us -> none  [on_device(): gathered = lax.all_gather(rhs_field, 'rows', axis=1, tiled=True)]
    pallas_call x0 -> x1, Pallas kernels: none -> 15.1 us  [on_device(): pl.pallas_call(functools.partial(kernel, n_rows, n_cols), out_shape=jax.S...]
    unnamed x4 -> x19, local copies, waits for them, and re-layouts: 0.01 us -> 9.06 us
  transfers between devices with their start and end apart: 1 -> 0, of which waited for: 1 -> 0; matrix products, arithmetic and copies ran while one was open for 0% -> 0% of each run, Pallas kernels for 0% -> 0%
where the time goes in v1:
time: 25.1 us; the launch traced here: 24.8 us
  Pallas kernels  15.1 us (60%)
  local copies, waits for them, and re-layouts  9.06 us (36%)
  between operations  0.68 us (3%)
    pallas_call x1, Pallas kernels, on_device(): pl.pallas_call(functools.partial(kernel, n_rows, n_cols), out_shape=jax.S...  15.1 us
    unnamed x19, local copies, waits for them, and re-layouts  9.06 us

profile of v1, /device:TPU:0, one launch (start us, length us, event | category | flops | bytes accessed | tf_op | source)
XLA Modules:
  0.0 24.8 jit_solution(12877719882875696953)
XLA Ops:
  0.7 0.0 copy-start
  0.7 1.6 %copy-done = bf16[1,64,64,256]{3,2,1,0:T(8,128)(2,1)S(1)} copy-done((bf16[1,64,64,256]{3,2,1,0:T(8,128)(2,1)S(1)}, bf16[1,64,64,256]{3,2,1,0:T(8,128)(2,1)}, u32[]{:S(2)}) %copy-start) | copy-done | bytes 2097176
  2.2 0.0 copy-start.1
  2.2 1.6 %copy-done.1 = bf16[1,64,64,256]{3,2,1,0:T(8,128)(2,1)S(1)} copy-done((bf16[1,64,64,256]{3,2,1,0:T(8,128)(2,1)S(1)}, bf16[1,64,64,256]{3,2,1,0:T(8,128)(2,1)}, u32[]{:S(2)}) %copy-start.1) | copy-done | bytes 2097176
  3.8 0.0 copy-start.2
  3.8 1.2 %copy-done.2 = bf16[1,8,256,256]{3,2,1,0:T(8,128)(2,1)S(1)} copy-done((bf16[1,8,256,256]{3,2,1,0:T(8,128)(2,1)S(1)}, bf16[1,8,256,256]{3,2,1,0:T(8,128)(2,1)}, u32[]{:S(2)}) %copy-start.2) | copy-done | bytes 1048600
  5.1 0.0 copy-start.3
  5.1 0.8 %copy-done.3 = bf16[64,256]{1,0:T(8,128)(2,1)S(1)} copy-done((bf16[64,256]{1,0:T(8,128)(2,1)S(1)}, bf16[64,256]{1,0:T(8,128)(2,1)}, u32[]{:S(2)}) %copy-start.3) | copy-done | bytes 32792
  5.8 0.0 copy-start.4
  5.8 0.7 %copy-done.4 = s32[1,64]{1,0:T(1,128)S(1)} copy-done((s32[1,64]{1,0:T(1,128)S(1)}, s32[1,64]{1,0:T(1,128)}, u32[]{:S(2)}) %copy-start.4) | copy-done | bytes 280
  6.5 0.0 copy-start.5
  6.5 0.7 %copy-done.5 = s32[1,64]{1,0:T(1,128)S(1)} copy-done((s32[1,64]{1,0:T(1,128)S(1)}, s32[1,64]{1,0:T(1,128)}, u32[]{:S(2)}) %copy-start.5) | copy-done | bytes 280
  7.1 0.0 copy-start.6
  7.1 0.7 %copy-done.6 = s32[1,64]{1,0:T(1,128)S(1)} copy-done((s32[1,64]{1,0:T(1,128)S(1)}, s32[1,64]{1,0:T(1,128)}, u32[]{:S(2)}) %copy-start.6) | copy-done | bytes 280
  7.8 0.0 copy-start.7
  7.8 0.7 %copy-done.7 = s32[1,8]{1,0:T(1,128)S(1)} copy-done((s32[1,8]{1,0:T(1,128)S(1)}, s32[1,8]{1,0:T(1,128)}, u32[]{:S(2)}) %copy-start.7) | copy-done | bytes 56
  8.4 0.0 copy-start.8
  8.4 0.7 %copy-done.8 = s32[1,8]{1,0:T(1,128)S(1)} copy-done((s32[1,8]{1,0:T(1,128)S(1)}, s32[1,8]{1,0:T(1,128)}, u32[]{:S(2)}) %copy-start.8) | copy-done | bytes 56
  9.1 15.1 %shard_map.100 = f32[64,256]{1,0:T(8,128)S(1)} custom-call(bf16[64,256]{1,0:T(8,128)(2,1)S(1)} %copy-done.3, bf16[1,64,64,256]{3,2,1,0:T(8,128)(2,1)S(1)} %copy-done, bf16[1,64,64,256]{3,2,1,0:T(8,128)(2,1)S(1)} %copy-done.1, s32[1,64]{1,0:T(1,128)S(1)} %copy-done.4, s32[1,64]{1,0:T(1,128)S(1)} %copy-done.5, s32[1,64]{1,0:T(1,128)S(1)} %copy-done.6, ...), custom_call_target="tpu_custom_call" | custom-call | tf_op jit(solution)/shard_map/pallas_call | solution.py:162
  24.2 0.6 %copy.13 = f32[64,256]{1,0:T(8,128)} copy(f32[64,256]{1,0:T(8,128)S(1)} %shard_map.100) | data formatting | bytes 131072
Async XLA Ops:
  0.7 1.6 %copy-start = (bf16[1,64,64,256]{3,2,1,0:T(8,128)(2,1)S(1)}, bf16[1,64,64,256]{3,2,1,0:T(8,128)(2,1)}, u32[]{:S(2)}) copy-start(bf16[1,64,64,256]{3,2,1,0:T(8,128)(2,1)} %left_ref.1) | copy-start | bytes 6291460
  2.2 1.6 %copy-start.1 = (bf16[1,64,64,256]{3,2,1,0:T(8,128)(2,1)S(1)}, bf16[1,64,64,256]{3,2,1,0:T(8,128)(2,1)}, u32[]{:S(2)}) copy-start(bf16[1,64,64,256]{3,2,1,0:T(8,128)(2,1)} %right_ref.1) | copy-start | bytes 6291460
  3.8 1.2 %copy-start.2 = (bf16[1,8,256,256]{3,2,1,0:T(8,128)(2,1)S(1)}, bf16[1,8,256,256]{3,2,1,0:T(8,128)(2,1)}, u32[]{:S(2)}) copy-start(bf16[1,8,256,256]{3,2,1,0:T(8,128)(2,1)} %near_ref.1) | copy-start | bytes 3145732
  5.1 0.8 %copy-start.3 = (bf16[64,256]{1,0:T(8,128)(2,1)S(1)}, bf16[64,256]{1,0:T(8,128)(2,1)}, u32[]{:S(2)}) copy-start(bf16[64,256]{1,0:T(8,128)(2,1)} %x_ref.1) | copy-start | bytes 98308
  5.8 0.7 %copy-start.4 = (s32[1,64]{1,0:T(1,128)S(1)}, s32[1,64]{1,0:T(1,128)}, u32[]{:S(2)}) copy-start(s32[1,64]{1,0:T(1,128)} %far_rows_ref.1) | copy-start | bytes 772
  6.5 0.7 %copy-start.5 = (s32[1,64]{1,0:T(1,128)S(1)}, s32[1,64]{1,0:T(1,128)}, u32[]{:S(2)}) copy-start(s32[1,64]{1,0:T(1,128)} %far_cols_ref.1) | copy-start | bytes 772
  7.1 0.7 %copy-start.6 = (s32[1,64]{1,0:T(1,128)S(1)}, s32[1,64]{1,0:T(1,128)}, u32[]{:S(2)}) copy-start(s32[1,64]{1,0:T(1,128)} %far_ranks_ref.1) | copy-start | bytes 772
  7.8 0.7 %copy-start.7 = (s32[1,8]{1,0:T(1,128)S(1)}, s32[1,8]{1,0:T(1,128)}, u32[]{:S(2)}) copy-start(s32[1,8]{1,0:T(1,128)} %near_rows_ref.1) | copy-start | bytes 100
  8.4 0.7 %copy-start.8 = (s32[1,8]{1,0:T(1,128)S(1)}, s32[1,8]{1,0:T(1,128)}, u32[]{:S(2)}) copy-start(s32[1,8]{1,0:T(1,128)} %near_cols_ref.1) | copy-start | bytes 100

commit v2 on v1

--- a/solution.py
+++ b/solution.py
@@ -30,7 +30,14 @@
     near,
     outgoing,
     incoming,
+    far_rows,
+    far_cols,
+    far_ranks,
+    far_counts,
+    near_rows,
+    near_cols,
     local_sem,
+    small_sem,
     send_sem,
     recv_sem,
     pair_sem,
@@ -47,6 +54,20 @@
         pltpu.make_async_copy(near_ref.at[0], near, local_sem.at[2]),
         pltpu.make_async_copy(left_ref.at[0], left, local_sem.at[3]),
     ]
+    small = [
+        pltpu.make_async_copy(source, target, small_sem.at[place])
+        for place, (source, target) in enumerate(
+            [
+                (far_rows_ref, far_rows),
+                (far_cols_ref, far_cols),
+                (far_ranks_ref, far_ranks),
+                (far_counts_ref, far_counts),
+                (near_rows_ref, near_rows),
+                (near_cols_ref, near_cols),
+            ]
+        )
+    ]
+    loads = small + loads
     for load in loads:
         load.start()
 
@@ -83,11 +104,11 @@
     for load in loads:
         load.wait()
 
-    live = far_counts_ref[0]
+    live = far_counts[0, 0]
     acc = jnp.zeros((2 * rhs, leaf), jnp.float32)
     for slot in range(near_slots):
-        piece = x_all[near_cols_ref[0, slot] // n_cols]
-        mine = near_rows_ref[0, slot] % n_cols == col
+        piece = x_all[near_cols[0, slot] // n_cols]
+        mine = near_rows[0, slot] % n_cols == col
         empty = jnp.zeros_like(piece)
         both = jnp.concatenate([jnp.where(mine, piece, empty), jnp.where(mine, empty, piece)], axis=0)
         acc += jnp.dot(both, near[slot], preferred_element_type=jnp.float32)
@@ -101,17 +122,17 @@
         for a in range(start, start + group, 2):
             b = a + 1
             pieces = jnp.concatenate(
-                [x_all[far_cols_ref[0, a] // n_cols], x_all[far_cols_ref[0, b] // n_cols]], axis=0
+                [x_all[far_cols[0, a] // n_cols], x_all[far_cols[0, b] // n_cols]], axis=0
             )
             weights = right[a : a + 2].reshape(width, leaf)
             scores = lax.dot_general(
                 pieces, weights, (((1,), (1,)), ((), ())), preferred_element_type=jnp.float32
             )
             scores = jnp.where(first, scores[:rhs], scores[rhs:])
-            end_a = jnp.where(a < live, far_ranks_ref[0, a], 0)
-            end_b = jnp.where(b < live, far_ranks_ref[0, b], 0) + rank
-            mine_a = far_rows_ref[0, a] % n_cols == col
-            mine_b = far_rows_ref[0, b] % n_cols == col
+            end_a = jnp.where(a < live, far_ranks[0, a], 0)
+            end_b = jnp.where(b < live, far_ranks[0, b], 0) + rank
+            mine_a = far_rows[0, a] % n_cols == col
+            mine_b = far_rows[0, b] % n_cols == col
             own = lane < jnp.where(first, jnp.where(mine_a, end_a, 0), jnp.where(mine_b, end_b, 0))
             other = lane < jnp.where(first, jnp.where(mine_a, 0, end_a), jnp.where(mine_b, 0, end_b))
             halves.append(
@@ -157,23 +178,11 @@
     near_cols,
 ):
     rhs, leaf = rhs_field.shape
-    anywhere = pl.BlockSpec(memory_space=pl.ANY)
-    scalars = pl.BlockSpec(memory_space=pltpu.SMEM)
+    in_hbm = pl.BlockSpec(memory_space=pltpu.HBM)
     return pl.pallas_call(
         functools.partial(kernel, n_rows, n_cols),
         out_shape=jax.ShapeDtypeStruct((rhs, leaf), jnp.float32),
-        in_specs=[
-            anywhere,
-            anywhere,
-            anywhere,
-            scalars,
-            scalars,
-            scalars,
-            scalars,
-            anywhere,
-            scalars,
-            scalars,
-        ],
+        in_specs=[in_hbm] * 10,
         out_specs=pl.BlockSpec(memory_space=pltpu.VMEM),
         scratch_shapes=[
             pltpu.VMEM((n_rows, rhs, leaf), jnp.bfloat16),
@@ -182,13 +191,20 @@
             pltpu.VMEM(near_blocks.shape[1:], jnp.bfloat16),
             pltpu.VMEM((rhs, leaf), jnp.float32),
             pltpu.VMEM((rhs, leaf), jnp.float32),
+            pltpu.SMEM(far_rows.shape, jnp.int32),
+            pltpu.SMEM(far_cols.shape, jnp.int32),
+            pltpu.SMEM(far_ranks.shape, jnp.int32),
+            pltpu.SMEM((1, 1), jnp.int32),
+            pltpu.SMEM(near_rows.shape, jnp.int32),
+            pltpu.SMEM(near_cols.shape, jnp.int32),
             pltpu.SemaphoreType.DMA((4,)),
+            pltpu.SemaphoreType.DMA((6,)),
             pltpu.SemaphoreType.DMA((n_rows,)),
             pltpu.SemaphoreType.DMA((n_rows,)),
             pltpu.SemaphoreType.DMA((2,)),
         ],
         compiler_params=pltpu.CompilerParams(
-            collective_id=0, has_side_effects=True, vmem_limit_bytes=32 * 1024 * 1024
+            collective_id=0, has_side_effects=True, vmem_limit_bytes=60 * 1024 * 1024
         ),
     )(
         rhs_field,
@@ -197,7 +213,7 @@
         far_rows,
         far_cols,
         far_ranks,
-        far_counts,
+        far_counts.reshape(1, 1),
         near_blocks,
         near_rows,
         near_cols,

time: 25.1 us -> 17.3 us (0.69)
  local copies, waits for them, and re-layouts: 9.06 us -> 1.47 us
    unnamed x19 -> x1, local copies, waits for them, and re-layouts: 9.06 us -> 1.47 us
where the time goes in v2:
time: 17.3 us; the launch traced here: 17.1 us
  Pallas kernels  15 us (87%)
  local copies, waits for them, and re-layouts  1.47 us (8%)
  between operations  0.66 us (4%)
    pallas_call x1, Pallas kernels, on_device(): pl.pallas_call(functools.partial(kernel, n_rows, n_cols), out_shape=jax.S...  15 us
    unnamed x1, local copies, waits for them, and re-layouts  1.47 us

profile of v2, /device:TPU:0, one launch (start us, length us, event | category | flops | bytes accessed | tf_op | source)
XLA Modules:
  0.0 17.1 jit_solution(1058424343439322203)
XLA Ops:
  0.7 15.0 %shard_map.100 = f32[64,256]{1,0:T(8,128)} custom-call(bf16[64,256]{1,0:T(8,128)(2,1)} %x_ref.1, bf16[1,64,64,256]{3,2,1,0:T(8,128)(2,1)} %left_ref.1, bf16[1,64,64,256]{3,2,1,0:T(8,128)(2,1)} %right_ref.1, s32[1,64]{1,0:T(1,128)} %far_rows_ref.1, s32[1,64]{1,0:T(1,128)} %far_cols_ref.1, s32[1,64]{1,0:T(1,128)} %far_ranks_ref.1, ...), custom_call_target="tpu_custom_call" | custom-call | tf_op jit(solution)/shard_map/pallas_call | solution.py:182
  15.7 1.5 %copy.13 = f32[64,256]{1,0:T(8,128)} copy(f32[64,256]{1,0:T(8,128)} %shard_map.100) | data formatting | bytes 131072

commit v3 on v2

--- a/solution.py
+++ b/solution.py
@@ -33,7 +33,6 @@
     far_rows,
     far_cols,
     far_ranks,
-    far_counts,
     near_rows,
     near_cols,
     local_sem,
@@ -61,7 +60,6 @@
                 (far_rows_ref, far_rows),
                 (far_cols_ref, far_cols),
                 (far_ranks_ref, far_ranks),
-                (far_counts_ref, far_counts),
                 (near_rows_ref, near_rows),
                 (near_cols_ref, near_cols),
             ]
@@ -104,7 +102,7 @@
     for load in loads:
         load.wait()
 
-    live = far_counts[0, 0]
+    live = far_counts_ref[0]
     acc = jnp.zeros((2 * rhs, leaf), jnp.float32)
     for slot in range(near_slots):
         piece = x_all[near_cols[0, slot] // n_cols]
@@ -178,11 +176,26 @@
     near_cols,
 ):
     rhs, leaf = rhs_field.shape
+    def stay(operand):
+        return pltpu.with_memory_space_constraint(operand, pltpu.HBM)
+
+    operands = [
+        stay(rhs_field),
+        stay(far_left),
+        stay(far_right),
+        stay(far_rows),
+        stay(far_cols),
+        stay(far_ranks),
+        far_counts,
+        stay(near_blocks),
+        stay(near_rows),
+        stay(near_cols),
+    ]
     in_hbm = pl.BlockSpec(memory_space=pltpu.HBM)
     return pl.pallas_call(
         functools.partial(kernel, n_rows, n_cols),
         out_shape=jax.ShapeDtypeStruct((rhs, leaf), jnp.float32),
-        in_specs=[in_hbm] * 10,
+        in_specs=[in_hbm] * 6 + [pl.BlockSpec(memory_space=pltpu.SMEM)] + [in_hbm] * 3,
         out_specs=pl.BlockSpec(memory_space=pltpu.VMEM),
         scratch_shapes=[
             pltpu.VMEM((n_rows, rhs, leaf), jnp.bfloat16),
@@ -194,30 +207,18 @@
             pltpu.SMEM(far_rows.shape, jnp.int32),
             pltpu.SMEM(far_cols.shape, jnp.int32),
             pltpu.SMEM(far_ranks.shape, jnp.int32),
-            pltpu.SMEM((1, 1), jnp.int32),
             pltpu.SMEM(near_rows.shape, jnp.int32),
             pltpu.SMEM(near_cols.shape, jnp.int32),
             pltpu.SemaphoreType.DMA((4,)),
-            pltpu.SemaphoreType.DMA((6,)),
+            pltpu.SemaphoreType.DMA((5,)),
             pltpu.SemaphoreType.DMA((n_rows,)),
             pltpu.SemaphoreType.DMA((n_rows,)),
             pltpu.SemaphoreType.DMA((2,)),
         ],
         compiler_params=pltpu.CompilerParams(
-            collective_id=0, has_side_effects=True, vmem_limit_bytes=60 * 1024 * 1024
+            collective_id=0, has_side_effects=True, vmem_limit_bytes=32 * 1024 * 1024
         ),
-    )(
-        rhs_field,
-        far_left,
-        far_right,
-        far_rows,
-        far_cols,
-        far_ranks,
-        far_counts.reshape(1, 1),
-        near_blocks,
-        near_rows,
-        near_cols,
-    )
+    )(*operands)
 
 
 def solution(mesh):

time: 17.3 us -> 15.8 us (0.913)
  local copies, waits for them, and re-layouts: 1.47 us -> 0.63 us
  Pallas kernels: 15 us -> 14.4 us
    unnamed x1, local copies, waits for them, and re-layouts: 1.47 us -> 0.63 us
    pallas_call x1, Pallas kernels: 15 us -> 14.4 us  [on_device(): pl.pallas_call(functools.partial(kernel, n_rows, n_cols), out_shape=jax.S...]
where the time goes in v3:
time: 15.8 us; the launch traced here: 15.7 us
  Pallas kernels  14.4 us (91%)
  between operations  0.66 us (4%)
  local copies, waits for them, and re-layouts  0.63 us (4%)
    pallas_call x1, Pallas kernels, on_device(): pl.pallas_call(functools.partial(kernel, n_rows, n_cols), out_shape=jax.S...  14.4 us
    unnamed x1, local copies, waits for them, and re-layouts  0.63 us

profile of v3, /device:TPU:0, one launch (start us, length us, event | category | flops | bytes accessed | tf_op | source)
XLA Modules:
  0.0 15.7 jit_solution(3694302804318519667)
XLA Ops:
  0.7 14.4 %shard_map.100 = f32[64,256]{1,0:T(8,128)S(1)} custom-call(bf16[64,256]{1,0:T(8,128)(2,1)} %x_ref.1, bf16[1,64,64,256]{3,2,1,0:T(8,128)(2,1)} %left_ref.1, bf16[1,64,64,256]{3,2,1,0:T(8,128)(2,1)} %right_ref.1, s32[1,64]{1,0:T(1,128)} %far_rows_ref.1, s32[1,64]{1,0:T(1,128)} %far_cols_ref.1, s32[1,64]{1,0:T(1,128)} %far_ranks_ref.1, ...), custom_call_target="tpu_custom_call" | custom-call | tf_op jit(solution)/shard_map/pallas_call | solution.py:195
  15.0 0.6 %copy.13 = f32[64,256]{1,0:T(8,128)} copy(f32[64,256]{1,0:T(8,128)S(1)} %shard_map.100) | data formatting | bytes 131072

commit v4 on v3

v4 whole, which is shorter than its diff:
```python
import functools

import jax
import jax.numpy as jnp
from jax import lax
from jax.experimental import pallas as pl
from jax.experimental.pallas import tpu as pltpu
from jax.sharding import PartitionSpec as P

MESH = pl.DeviceIdType.MESH


def kernel(
    n_rows,
    n_cols,
    x_ref,
    left_ref,
    right_ref,
    far_rows_ref,
    far_cols_ref,
    far_ranks_ref,
    far_counts_ref,
    near_ref,
    near_rows_ref,
    near_cols_ref,
    out_ref,
    x_all,
    left,
    right,
    near,
    outgoing,
    incoming,
    far_rows,
    far_cols,
    far_ranks,
    near_rows,
    near_cols,
    here_sem,
    local_sem,
    small_sem,
    send_sem,
    recv_sem,
    pair_sem,
):
    row = lax.axis_index("rows")
    col = lax.axis_index("cols")
    far_slots, rank, leaf = right.shape
    near_slots = near.shape[0]
    pieces, _, rhs, _ = x_all.shape

    small = [
        pltpu.make_async_copy(source, target, small_sem.at[place])
        for place, (source, target) in enumerate(
            [
                (far_rows_ref, far_rows),
                (far_cols_ref, far_cols),
                (far_ranks_ref, far_ranks),
                (near_rows_ref, near_rows),
                (near_cols_ref, near_cols),
            ]
        )
    ]
    large = [
        pltpu.make_async_copy(right_ref.at[0], right, local_sem.at[0]),
        pltpu.make_async_copy(near_ref.at[0], near, local_sem.at[1]),
        pltpu.make_async_copy(left_ref.at[0], left, local_sem.at[2]),
    ]
    here = [
        pltpu.make_async_copy(
            x_ref.at[piece * rhs : (piece + 1) * rhs], x_all.at[piece, row], here_sem.at[piece]
        )
        for piece in range(pieces)
    ]
    loads = here + small + large
    for load in loads:
        load.start()

    peers = [
        (lax.rem(row + offset, n_rows), lax.rem(row + n_rows - offset, n_rows))
        for offset in range(1, n_rows)
    ]
    barrier = pltpu.get_barrier_semaphore()
    for target, _ in peers:
        pl.semaphore_signal(barrier, inc=1, device_id={"rows": target}, device_id_type=MESH)
    pl.semaphore_signal(barrier, inc=1, device_id={"cols": 1 - col}, device_id_type=MESH)
    pl.semaphore_wait(barrier, n_rows)

    def push(piece, number, origin, target):
        return pltpu.make_async_remote_copy(
            src_ref=x_ref.at[piece * rhs : (piece + 1) * rhs],
            dst_ref=x_all.at[piece, origin],
            send_sem=send_sem.at[piece, number],
            recv_sem=recv_sem.at[piece, number],
            device_id={"rows": target},
            device_id_type=MESH,
        )

    sends = []
    for piece in range(pieces):
        for number, (target, _) in enumerate(peers):
            sends.append(push(piece, number, row, target))
            sends[-1].start()
    for load in loads:
        load.wait()

    live = far_counts_ref[0]
    width = 2 * rank
    lane = lax.broadcasted_iota(jnp.int32, (1, width), 1)
    first = lane < rank
    exchanges = []
    for piece in range(pieces):
        for number, (target, source) in enumerate(peers):
            push(piece, number, source, target).wait_recv()

        acc = jnp.zeros((2 * rhs, leaf), jnp.float32)
        for slot in range(near_slots):
            block = x_all[piece, near_cols[0, slot] // n_cols]
            mine = near_rows[0, slot] % n_cols == col
            empty = jnp.zeros_like(block)
            both = jnp.concatenate(
                [jnp.where(mine, block, empty), jnp.where(mine, empty, block)], axis=0
            )
            acc += jnp.dot(both, near[slot], preferred_element_type=jnp.float32)

        coefficients = []
        for start in range(0, far_slots, 2):
            slots = range(start, start + 2)
            blocks = jnp.concatenate(
                [x_all[piece, far_cols[0, slot] // n_cols] for slot in slots], axis=0
            )
            scores = lax.dot_general(
                blocks,
                right[start : start + 2].reshape(2 * rank, leaf),
                (((1,), (1,)), ((), ())),
                preferred_element_type=jnp.float32,
            )
            for place in range(0, 2, 2):
                a, b = start + place, start + place + 1
                columns = scores[:, place * rank : (place + 2) * rank]
                kept = jnp.where(
                    first,
                    columns[place * rhs : (place + 1) * rhs],
                    columns[(place + 1) * rhs : (place + 2) * rhs],
                )
                end_a = jnp.where(a < live, far_ranks[0, a], 0)
                end_b = jnp.where(b < live, far_ranks[0, b], 0) + rank
                mine_a = far_rows[0, a] % n_cols == col
                mine_b = far_rows[0, b] % n_cols == col
                own = lane < jnp.where(
                    first, jnp.where(mine_a, end_a, 0), jnp.where(mine_b, end_b, 0)
                )
                other = lane < jnp.where(
                    first, jnp.where(mine_a, 0, end_a), jnp.where(mine_b, 0, end_b)
                )
                coefficients.append(
                    jnp.concatenate(
                        [jnp.where(own, kept, 0.0), jnp.where(other, kept, 0.0)], axis=0
                    ).astype(jnp.bfloat16)
                )
        acc += jnp.dot(
            jnp.concatenate(coefficients, axis=1),
            left[...].reshape(far_slots * rank, leaf),
            preferred_element_type=jnp.float32,
        )

        outgoing[piece] = acc[rhs:]
        exchanges.append(
            pltpu.make_async_remote_copy(
                src_ref=outgoing.at[piece],
                dst_ref=incoming.at[piece],
                send_sem=pair_sem.at[0, piece],
                recv_sem=pair_sem.at[1, piece],
                device_id={"cols": 1 - col},
                device_id_type=MESH,
            )
        )
        exchanges[-1].start()
        out_ref[piece * rhs : (piece + 1) * rhs] = acc[:rhs]

    for copy in sends:
        copy.wait_send()
    for piece in range(pieces):
        exchanges[piece].wait()
        out_ref[piece * rhs : (piece + 1) * rhs] += incoming[piece]


def on_device(
    n_rows,
    n_cols,
    rhs_field,
    far_left,
    far_right,
    far_rows,
    far_cols,
    far_ranks,
    far_counts,
    near_blocks,
    near_rows,
    near_cols,
):
    rhs, leaf = rhs_field.shape
    pieces = 1
    def stay(operand):
        return pltpu.with_memory_space_constraint(operand, pltpu.HBM)

    operands = [
        stay(rhs_field),
        stay(far_left),
        stay(far_right),
        stay(far_rows),
        stay(far_cols),
        stay(far_ranks),
        far_counts,
        stay(near_blocks),
        stay(near_rows),
        stay(near_cols),
    ]
    in_hbm = pl.BlockSpec(memory_space=pltpu.HBM)
    return pl.pallas_call(
        functools.partial(kernel, n_rows, n_cols),
        out_shape=jax.ShapeDtypeStruct((rhs, leaf), jnp.float32),
        in_specs=[in_hbm] * 6 + [pl.BlockSpec(memory_space=pltpu.SMEM)] + [in_hbm] * 3,
        out_specs=pl.BlockSpec(memory_space=pltpu.VMEM),
        scratch_shapes=[
            pltpu.VMEM((pieces, n_rows, rhs // pieces, leaf), jnp.bfloat16),
            pltpu.VMEM(far_left.shape[1:], jnp.bfloat16),
            pltpu.VMEM(far_right.shape[1:], jnp.bfloat16),
            pltpu.VMEM(near_blocks.shape[1:], jnp.bfloat16),
            pltpu.VMEM((pieces, rhs // pieces, leaf), jnp.float32),
            pltpu.VMEM((pieces, rhs // pieces, leaf), jnp.float32),
            pltpu.SMEM(far_rows.shape, jnp.int32),
            pltpu.SMEM(far_cols.shape, jnp.int32),
            pltpu.SMEM(far_ranks.shape, jnp.int32),
            pltpu.SMEM(near_rows.shape, jnp.int32),
            pltpu.SMEM(near_cols.shape, jnp.int32),
            pltpu.SemaphoreType.DMA((pieces,)),
            pltpu.SemaphoreType.DMA((3,)),
            pltpu.SemaphoreType.DMA((5,)),
            pltpu.SemaphoreType.DMA((pieces, n_rows)),
            pltpu.SemaphoreType.DMA((pieces, n_rows)),
            pltpu.SemaphoreType.DMA((2, pieces)),
        ],
        compiler_params=pltpu.CompilerParams(
            collective_id=0, has_side_effects=True, vmem_limit_bytes=32 * 1024 * 1024
        ),
    )(*operands)


def solution(mesh):
    split = ("groups", "rows", "cols")
    placed = (
        P(None, split),
        P(split, None, None, None),
        P(split, None, None, None),
        P(split, None),
        P(split, None),
        P(split, None),
        P(split),
        P(split, None, None, None),
        P(split, None),
        P(split, None),
    )
    return jax.shard_map(
        functools.partial(on_device, mesh.shape["rows"], mesh.shape["cols"]),
        mesh=mesh,
        in_specs=placed,
        out_specs=P(None, split),
        check_vma=False,
    )
```

time: 15.8 us -> 15.2 us (0.962)
  Pallas kernels: 14.4 us -> 13.7 us
    pallas_call x1, Pallas kernels: 14.4 us -> 13.7 us  [on_device(): pl.pallas_call(functools.partial(kernel, n_rows, n_cols), out_shape=jax.S...]
where the time goes in v4:
time: 15.2 us; the launch traced here: 15 us
  Pallas kernels  13.7 us (90%)
  between operations  0.66 us (4%)
  local copies, waits for them, and re-layouts  0.63 us (4%)
    pallas_call x1, Pallas kernels, on_device(): pl.pallas_call(functools.partial(kernel, n_rows, n_cols), out_shape=jax.S...  13.7 us
    unnamed x1, local copies, waits for them, and re-layouts  0.63 us

profile of v4, /device:TPU:0, one launch (start us, length us, event | category | flops | bytes accessed | tf_op | source)
XLA Modules:
  0.0 15.0 jit_solution(12702209539268792160)
XLA Ops:
  0.7 13.7 %shard_map.100 = f32[64,256]{1,0:T(8,128)S(1)} custom-call(bf16[64,256]{1,0:T(8,128)(2,1)} %x_ref.1, bf16[1,64,64,256]{3,2,1,0:T(8,128)(2,1)} %left_ref.1, bf16[1,64,64,256]{3,2,1,0:T(8,128)(2,1)} %right_ref.1, s32[1,64]{1,0:T(1,128)} %far_rows_ref.1, s32[1,64]{1,0:T(1,128)} %far_cols_ref.1, s32[1,64]{1,0:T(1,128)} %far_ranks_ref.1, ...), custom_call_target="tpu_custom_call" | custom-call | tf_op jit(solution)/shard_map/pallas_call | solution.py:219
  14.4 0.6 %copy.13 = f32[64,256]{1,0:T(8,128)} copy(f32[64,256]{1,0:T(8,128)S(1)} %shard_map.100) | data formatting | bytes 131072

commit v5 on v4

--- a/solution.py
+++ b/solution.py
@@ -109,18 +109,27 @@
     first = lane < rank
     exchanges = []
     for piece in range(pieces):
-        for number, (target, source) in enumerate(peers):
-            push(piece, number, source, target).wait_recv()
+        arrivals = [
+            push(piece, number, source, target) for number, (target, source) in enumerate(peers)
+        ]
+        arrivals[0].wait_recv()
+        arrivals[-1].wait_recv()
 
         acc = jnp.zeros((2 * rhs, leaf), jnp.float32)
+        below, above = lax.rem(row + n_rows - 1, n_rows), lax.rem(row + 1, n_rows)
+        beside = [x_all[piece, below], x_all[piece, row], x_all[piece, above]]
         for slot in range(near_slots):
-            block = x_all[piece, near_cols[0, slot] // n_cols]
+            key = near_cols[0, slot] // n_cols
+            block = jnp.where(key < row, beside[0], jnp.where(key == row, beside[1], beside[2]))
             mine = near_rows[0, slot] % n_cols == col
             empty = jnp.zeros_like(block)
             both = jnp.concatenate(
                 [jnp.where(mine, block, empty), jnp.where(mine, empty, block)], axis=0
             )
             acc += jnp.dot(both, near[slot], preferred_element_type=jnp.float32)
+
+        for arrival in arrivals[1:-1]:
+            arrival.wait_recv()
 
         coefficients = []
         for start in range(0, far_slots, 2):

time: 15.2 us -> 15.1 us (level)
    pallas_call x1, Pallas kernels: 13.7 us -> 13.6 us  [on_device(): pl.pallas_call(functools.partial(kernel, n_rows, n_cols), out_shape=jax.S...]
where the time goes in v5:
time: 15.1 us; the launch traced here: 14.9 us
  Pallas kernels  13.6 us (90%)
  between operations  0.66 us (4%)
  local copies, waits for them, and re-layouts  0.63 us (4%)
    pallas_call x1, Pallas kernels, on_device(): pl.pallas_call(functools.partial(kernel, n_rows, n_cols), out_shape=jax.S...  13.6 us
    unnamed x1, local copies, waits for them, and re-layouts  0.63 us

profile of v5, /device:TPU:0, one launch (start us, length us, event | category | flops | bytes accessed | tf_op | source)
XLA Modules:
  0.0 14.9 jit_solution(12334253864346904430)
XLA Ops:
  0.7 13.6 %shard_map.100 = f32[64,256]{1,0:T(8,128)S(1)} custom-call(bf16[64,256]{1,0:T(8,128)(2,1)} %x_ref.1, bf16[1,64,64,256]{3,2,1,0:T(8,128)(2,1)} %left_ref.1, bf16[1,64,64,256]{3,2,1,0:T(8,128)(2,1)} %right_ref.1, s32[1,64]{1,0:T(1,128)} %far_rows_ref.1, s32[1,64]{1,0:T(1,128)} %far_cols_ref.1, s32[1,64]{1,0:T(1,128)} %far_ranks_ref.1, ...), custom_call_target="tpu_custom_call" | custom-call | tf_op jit(solution)/shard_map/pallas_call | solution.py:228
  14.2 0.6 %copy.13 = f32[64,256]{1,0:T(8,128)} copy(f32[64,256]{1,0:T(8,128)S(1)} %shard_map.100) | data formatting | bytes 131072
